TPU v7x, 256 devices: a whole 4x4x8 slice. The times are simulated.
256 devices in a mesh: rep: 8 (over y, x_hi), blk: 32 (over z, x_lo, core).
Axes of the slice: x: 4 (x_hi: 2, x_lo: 2; x = x_hi * 2 + x_lo), y: 4, z: 8, core: 2. Of those that a mesh axis runs over, the one named last changes fastest.
Arguments:
- features: bfloat16 [65536, 128], P(('blk', 'rep')), may hold values from -6 to 6
- weight: bfloat16 [128, 256], replicated, may hold values from -0.5 to 0.5
- bias_vector: float32 [256], replicated, may hold values from -3 to 3
- adj_tiles: bfloat16 [32, 32, 16, 128, 128], P('blk', 'rep'), may hold values from -0.15625 to 0.15625
- tile_rows: int32 [32, 32, 16], P('blk', 'rep'), may hold values from 0 to 15
- tile_cols: int32 [32, 32, 16], P('blk', 'rep'), may hold values from 0 to 15
- counts: int32 [32, 32], P('blk', 'rep'), may hold values from 1 to 16, as said below
- cotangent: bfloat16 [65536, 256], P('blk'), may hold values from -6 to 6
Outputs:
- activations: bfloat16 [65536, 256], P('blk')
- feature_grad: float32 [65536, 128], P(('rep', 'blk'))
- weight_grad: float32 [128, 256], replicated
- bias_grad: float32 [256], replicated
Inputs may be any that keep to these rules, and one draw needn't show every extreme that they name: counts never exceeds 16, and some pair of blocks has exactly 16 live slots.
All inputs are finite; a program needn't handle non-finite values.
Results may differ from a plain program's by a relative error of at most 0.0055.
Values may be sent and summed in bfloat16 or wider, within the bound.
A program may use at most 64 MiB of HBM per device.

v0:
```python
import jax
import jax.numpy as jnp
from jax import lax
from jax.sharding import PartitionSpec as P


def slot_products(tile_part, source_blocks, fetch_index, put_index, live_mask, transpose):
    picked = jnp.take(source_blocks, fetch_index, axis=0)
    if transpose:
        products = jnp.einsum("cij,cif->cjf", tile_part, picked, preferred_element_type=jnp.float32)
    else:
        products = jnp.einsum("cij,cjf->cif", tile_part, picked, preferred_element_type=jnp.float32)
    masked = jnp.where(live_mask[:, None, None], products, jnp.zeros_like(products))
    return jnp.zeros(source_blocks.shape, jnp.float32).at[put_index].add(masked)


def section_sum(tile_set, source_blocks, fetch_index, put_index, live_count, transpose):
    slot_count = tile_set.shape[0]
    slot_index = lax.broadcasted_iota(jnp.int32, (slot_count,), 0)
    live_mask = slot_index < live_count
    return slot_products(tile_set, source_blocks, fetch_index, put_index, live_mask, transpose)


def on_device(features, weight, bias_vector, adj_tiles, tile_rows, tile_cols, counts, cotangent):
    n_rep = lax.axis_size("rep")
    rep_index = lax.axis_index("rep")
    sections = adj_tiles.shape[1]
    tile_side = adj_tiles.shape[3]
    own_panel = lax.all_gather(features, "rep", axis=0, tiled=True)
    slab_rows = own_panel.shape[0]
    feat_width = own_panel.shape[1]
    per_side = slab_rows // tile_side

    def forward_terms(section, source_panel):
        return section_sum(
            adj_tiles[0, section],
            source_panel.reshape(per_side, tile_side, feat_width),
            tile_cols[0, section],
            tile_rows[0, section],
            counts[0, section],
            False,
        ).reshape(slab_rows, feat_width)

    running_sum = jnp.zeros((slab_rows, feat_width), jnp.float32)
    everything = lax.all_gather(own_panel, "blk", axis=0, tiled=True)

    def one_section(section, running):
        first = (rep_index * sections + section) * slab_rows
        return running + forward_terms(
            section, lax.dynamic_slice_in_dim(everything, first, slab_rows, 0)
        )

    running_sum = lax.fori_loop(0, sections, one_section, running_sum)
    aggregated = lax.psum(running_sum, "rep")
    agg_low = aggregated.astype(jnp.bfloat16)
    preact = jnp.dot(agg_low, weight, preferred_element_type=jnp.float32) + bias_vector
    sigmoid_v = jax.nn.sigmoid(preact)
    activations = (preact * sigmoid_v).astype(jnp.bfloat16)
    grad_pre = cotangent.astype(jnp.float32) * sigmoid_v * (1.0 + preact * (1.0 - sigmoid_v))
    grad_low = grad_pre.astype(jnp.bfloat16)
    share = slab_rows // n_rep
    first_row = rep_index * share
    agg_share = lax.dynamic_slice_in_dim(agg_low, first_row, share, 0)
    grad_share = lax.dynamic_slice_in_dim(grad_low, first_row, share, 0)
    weight_part = lax.dot_general(
        agg_share, grad_share, (((0,), (0,)), ((), ())), preferred_element_type=jnp.float32
    )
    bias_part = jnp.sum(lax.dynamic_slice_in_dim(grad_pre, first_row, share, 0), axis=0)
    weight_grad, bias_grad = lax.psum((weight_part, bias_part), ("rep", "blk"))
    back_rows = lax.dot_general(
        grad_low, weight, (((1,), (1,)), ((), ())), preferred_element_type=jnp.float32
    ).astype(jnp.bfloat16)
    back_blocks = back_rows.reshape(per_side, tile_side, feat_width)

    def backward_section(section):
        return section_sum(
            adj_tiles[0, section],
            back_blocks,
            tile_rows[0, section],
            tile_cols[0, section],
            counts[0, section],
            True,
        ).reshape(slab_rows, feat_width)

    section_parts = lax.map(backward_section, jnp.arange(sections, dtype=jnp.int32))
    feature_grad = lax.psum_scatter(
        section_parts.reshape(sections * slab_rows, feat_width),
        "blk",
        scatter_dimension=0,
        tiled=True,
    )
    return (activations, feature_grad, weight_grad, bias_grad)


def solution(mesh):
    placed = (
        P(("blk", "rep"), None),
        P(),
        P(),
        P("blk", "rep", None, None, None),
        P("blk", "rep", None),
        P("blk", "rep", None),
        P("blk", "rep"),
        P("blk", None),
    )
    return jax.shard_map(
        on_device,
        mesh=mesh,
        in_specs=placed,
        out_specs=(P("blk", None), P(("rep", "blk"), None), P(), P()),
        check_vma=False,
    )
```

profile of v0, /device:TPU:1, one launch (start us, length us, event | category | flops | bytes accessed | tf_op | source)
XLA Modules:
  0.0 643.1 jit_solution(9114882994179825277)
XLA Ops:
  7.2 34.0 %all_gather.6 = bf16[2048,128]{1,0:T(8,128)(2,1)} all-gather(bf16[256,128]{1,0:T(8,128)(2,1)} %param.14), channel_id=1, replica_groups=mesh['rep'=8,'blk'=32] {'rep'}, dimensions={0}, use_global_device_ids=true | all-gather | bytes 589824 | tf_op jit(solution)/shard_map/all_gather | solution.py:29
  41.3 108.1 %all-gather.2.cloned.1.call-done = bf16[65536,128]{1,0:T(8,128)(2,1)} async-done(((bf16[2048,128]{1,0:T(8,128)(2,1)}), bf16[65536,128]{1,0:T(8,128)(2,1)}) %all-gather.2.cloned.1.call-update) | async-done | bytes 16777232 | tf_op jit(solution)/shard_map/all_gather | solution.py:45
  149.4 33.6 %while.27 = (s32[]{:T(128)}, f32[2048,128]{1,0:T(8,128)S(1)}, s32[1,4,16]{2,1,0:T(4,128)}, s32[1,4]{1,0:T(1,128)}, bf16[1,4,16,128,128]{4,3,2,1,0:T(8,128)(2,1)}...) while((s32[]{:T(128)}, f32[2048,128]{1,0:T(8,128)S(1)}, ...), condition=%wide.region_2.4_spmd.clone, body=%wide.region_0.3_spmd.clone.sunk | while | flops 68420776 | bytes 11539681 | solution.py:53
  149.4 1.1 constant_dynamic-slice_fusion.11
  150.5 1.2 constant_dynamic-slice_fusion.12
  151.8 1.3 compare_and_fusion.5
  153.8 1.4 convolution_select_fusion.5
  156.0 1.6 scatter_fusion.1
  157.8 1.1 constant_dynamic-slice_fusion.11
  158.9 1.2 constant_dynamic-slice_fusion.12
  160.2 1.3 compare_and_fusion.5
  162.2 1.4 convolution_select_fusion.5
  164.4 1.6 scatter_fusion.1
  166.2 1.1 constant_dynamic-slice_fusion.11
  167.3 1.2 constant_dynamic-slice_fusion.12
  168.6 1.3 compare_and_fusion.5
  170.6 1.4 convolution_select_fusion.5
  172.8 1.6 scatter_fusion.1
  174.6 1.1 constant_dynamic-slice_fusion.11
  175.7 1.2 constant_dynamic-slice_fusion.12
  177.0 1.3 compare_and_fusion.5
  179.0 1.4 convolution_select_fusion.5
  181.2 1.6 scatter_fusion.1
  183.0 76.1 %all-reduce.4 = bf16[2048,128]{1,0:T(8,128)(2,1)S(1)} all-reduce(f32[2048,128]{1,0:T(8,128)S(1)} %get-tuple-element.238), channel_id=1, replica_groups=mesh['rep'=8,'blk'=32] {'rep'}, use_global_device_ids=true, to_apply=%region_3.5 | all-reduce | flops 262144 | bytes 1572864 | tf_op jit(solution)/shard_map/psum | solution.py:54
  259.1 4.1 fusion.24
  263.7 0.9 fusion.20
  264.7 40.1 %while.26 = (s32[]{:T(128)}, f32[4,2048,128]{2,1,0:T(8,128)}, s32[4]{0:T(128)S(1)}, s32[1,4,16]{2,1,0:T(4,128)}, s32[1,4]{1,0:T(1,128)S(1)}, /*index=5*/bf16[1,4...) while((s32[]{:T(128)}, f32[4,2048,128]{2,1,0:T(8,128)}, ...), condition=%wide.region_6.8_spmd, body=%wide.region_4.7_spmd.sunk | while | flops 67896480 | bytes 9442499 | solution.py:85
  267.8 1.3 compare_and_fusion.4
  269.8 1.4 convolution_select_fusion.4
  272.0 1.6 scatter_fusion
  273.6 1.1 bitcast_dynamic-update-slice_fusion.2
  277.8 1.3 compare_and_fusion.4
  279.8 1.4 convolution_select_fusion.4
  282.0 1.6 scatter_fusion
  283.7 1.1 bitcast_dynamic-update-slice_fusion.2
  287.9 1.3 compare_and_fusion.4
  289.9 1.4 convolution_select_fusion.4
  292.1 1.6 scatter_fusion
  293.7 1.1 bitcast_dynamic-update-slice_fusion.2
  297.9 1.3 compare_and_fusion.4
  299.9 1.4 convolution_select_fusion.4
  302.1 1.6 scatter_fusion
  303.7 1.1 bitcast_dynamic-update-slice_fusion.2
  304.8 1.0 dynamic-slice_reduce_fusion
  305.8 86.7 %psum.23 = f32[256]{0:T(256)} all-reduce(f32[256]{0:T(256)S(1)} %dynamic-slice_reduce_fusion), channel_id=1, replica_groups=mesh['rep'=8,'blk'=32] {'rep','blk'}, use_global_device_ids=true, to_apply=%region_10.12 | all-reduce | flops 256 | bytes 2048 | tf_op jit(solution)/shard_map/psum | solution.py:69
  392.5 122.2 %all-reduce.3.cloned.1.call-done = f32[128,256]{1,0:T(8,128)} async-done(((f32[128,256]{1,0:T(8,128)}), f32[128,256]{1,0:T(8,128)}) %all-reduce.3.cloned.1.call-update) | async-done | bytes 131088 | tf_op jit(solution)/shard_map/psum | solution.py:69
  514.8 120.2 %reduce-scatter.2.cloned.1.call-done = f32[256,128]{1,0:T(8,128)} async-done(((f32[8192,128]{1,0:T(8,128)}), f32[256,128]{1,0:T(8,128)}) %reduce-scatter.2.cloned.1.call-update) | async-done | bytes 131088 | tf_op jit(solution)/shard_map/reduce_scatter | solution.py:86
  635.0 1.6 copy.32
  (60 shorter events, 17.6 us)
Async XLA Ops:
  7.2 252.0 %copy-start = (bf16[128,256]{1,0:T(8,128)(2,1)S(1)}, bf16[128,256]{1,0:T(8,128)(2,1)}, u32[]{:S(2)}) copy-start(bf16[128,256]{1,0:T(8,128)(2,1)} %param.15) | copy-start | bytes 196612
  7.2 142.2 %all-gather.2.cloned.1.call-start = ((), (), s32[]{:S(2)}) async-start(), calls=%async_computation.1 | async-start | bytes 17301504 | tf_op jit(solution)/shard_map/all_gather | solution.py:45
  41.2 473.6 %all-reduce.3.cloned.1.call-start = ((), (), s32[]{:S(2)}) async-start(), calls=%async_computation.3 | async-start | bytes 262144 | tf_op jit(solution)/shard_map/psum | solution.py:69
  149.4 109.7 %copy-start.1 = (f32[256]{0:T(256)S(1)}, f32[256]{0:T(256)}, u32[]{:S(2)}) copy-start(f32[256]{0:T(256)} %param.16) | copy-start | bytes 3076
  263.3 1.4 copy-start.2
  264.6 370.4 %reduce-scatter.2.cloned.1.call-start = ((), (), s32[]{:S(2)}) async-start(), calls=%async_computation.2 | async-start | bytes 4325376 | tf_op jit(solution)/shard_map/reduce_scatter | solution.py:86
Sparse Core Ops, SparseCore 0:
  41.4 108.0 all-gather.1
  264.7 250.0 all-reduce.2
  517.9 117.0 reduce-scatter.1
where the time goes:
time: 647 us; the launch traced here: 643 us
  waiting for transfers between devices  351 us (54%)
  blocking collectives  197 us (30%)
  other arithmetic  31 us (5%)
  local copies, waits for them, and re-layouts  25.8 us (4%)
  matrix products  16.8 us (3%)
  between operations  13.8 us (2%)
  loops' own time  8.21 us (1%)
    psum x1, waiting for transfers between devices, on_device(): weight_grad, bias_grad = lax.psum((weight_part, bias_part), ('rep', 'blk'))  122 us
    reduce_scatter x1, waiting for transfers between devices, on_device(): lax.psum_scatter(section_parts.reshape(sections * slab_rows, feat_width),...  120 us
    all_gather x1, waiting for transfers between devices, on_device(): everything = lax.all_gather(own_panel, 'blk', axis=0, tiled=True)  108 us
    psum x1, blocking collectives, on_device(): weight_grad, bias_grad = lax.psum((weight_part, bias_part), ('rep', 'blk'))  86.7 us
    psum x1, blocking collectives, on_device(): aggregated = lax.psum(running_sum, 'rep')  76.1 us
    all_gather x1, blocking collectives, on_device(): own_panel = lax.all_gather(features, 'rep', axis=0, tiled=True)  34 us
  transfers between devices with their start and end apart: 3, of which 3 were waited for; matrix products, arithmetic and copies ran while one was open for 5% of the time, Pallas kernels for 0%

commit v1 on v0

v1 whole, which is shorter than its diff:
```python
import functools

import jax
import jax.numpy as jnp
from jax import lax
from jax.experimental import pallas as pl
from jax.experimental.pallas import tpu as pltpu
from jax.sharding import PartitionSpec as P

MESH = pl.DeviceIdType.MESH
F32 = jnp.float32
BF16 = jnp.bfloat16
VMEM = pl.BlockSpec(memory_space=pltpu.VMEM)
SMEM = pl.BlockSpec(memory_space=pltpu.SMEM)
DMA = pltpu.SemaphoreType.DMA

REP = 8
BLK = 32
NZ = 8
SECTIONS = 4
CAP = 16
TILE = 128
PER_SIDE = 16
SLAB = 2048
SHARE = 256
F = 128
H = 256


def remote(src, dst, send_sem, recv_sem, device):
    return pltpu.make_async_remote_copy(
        src_ref=src,
        dst_ref=dst,
        send_sem=send_sem,
        recv_sem=recv_sem,
        device_id=device,
        device_id_type=MESH,
    )


def meet(peers):
    barrier = pltpu.get_barrier_semaphore()
    for peer in peers:
        pl.semaphore_signal(barrier, inc=1, device_id=peer, device_id_type=MESH)
    pl.semaphore_wait(barrier, len(peers))


def wrap(value, size):
    return lax.rem(value + size, size)


def place():
    rep = lax.axis_index("rep")
    blk = lax.axis_index("blk")
    z = blk // 4
    low = lax.rem(blk, 4)
    return rep, blk, z, low, low // 2, lax.rem(low, 2)


def gather_kernel(own_ref, out_ref, ring, zs, zr, ps, pr, cs, cr):
    rep, blk, z, low, xl, core = place()
    right = (rep, wrap(z + 1, NZ) * 4 + low)
    left = (rep, wrap(z - 1, NZ) * 4 + low)
    sibling = (rep, z * 4 + xl * 2 + (1 - core))

    def in_plane(to_rep, to_xl):
        return (to_rep, z * 4 + to_xl * 2 + core)

    peers = [right, left, sibling, (rep, z * 4 + (1 - xl) * 2 + core)]
    for step in range(1, REP):
        for to_xl in range(2):
            peers.append(in_plane(wrap(rep + step, REP), to_xl))
    meet(peers)

    started = []

    def start(copy):
        copy.start()
        started.append(copy)

    landing = out_ref.at[pl.ds(low * SLAB + rep * SHARE, SHARE)]

    def plane_copy(piece, slot, group, to_xl):
        return remote(piece, landing, ps.at[slot * 2 + to_xl], pr.at[rep * 2 + xl], in_plane(group, to_xl))

    def spread(piece, slot, group):
        for to_xl in range(2):
            here = (group == rep) & (xl == to_xl)

            @pl.when(here)
            def _():
                out_ref[pl.ds(low * SLAB + rep * SHARE, SHARE), :] = piece[...]

            @pl.when(jnp.logical_not(here))
            def _():
                plane_copy(piece, slot, group, to_xl).start()

    def slot_of(step, going_right):
        return step if going_right else 4 + step

    start(remote(own_ref, ring.at[slot_of(1, True)], zs.at[slot_of(1, True)], zr.at[slot_of(1, True)], right))
    start(remote(own_ref, ring.at[slot_of(1, False)], zs.at[slot_of(1, False)], zr.at[slot_of(1, False)], left))
    spread(own_ref, 0, z)
    pieces = [(own_ref, 0, z)]
    for step in range(1, 5):
        for going_right in (True, False):
            last = 4 if going_right else 3
            if step > last:
                continue
            slot = slot_of(step, going_right)
            towards = right if going_right else left
            remote(own_ref, ring.at[slot], zs.at[slot], zr.at[slot], towards).wait_recv()
            if step < last:
                following = slot_of(step + 1, going_right)
                start(remote(ring.at[slot], ring.at[following], zs.at[following], zr.at[following], towards))
            group = wrap(z - step if going_right else z + step, NZ)
            spread(ring.at[slot], slot, group)
            pieces.append((ring.at[slot], slot, group))

    for k in range(REP):
        q = wrap(rep + k, REP)
        for from_xl in range(2):
            index = q * 2 + from_xl
            rows = out_ref.at[pl.ds((from_xl * 2 + core) * SLAB + q * SHARE, SHARE)]
            if k == 0:

                @pl.when(xl != from_xl)
                def _():
                    remote(own_ref, rows, ps.at[0], pr.at[index], sibling).wait_recv()
            else:
                remote(own_ref, rows, ps.at[0], pr.at[index], sibling).wait_recv()
            start(remote(rows, rows, cs.at[index], cr.at[index], sibling))
    for k in range(REP):
        q = wrap(rep + k, REP)
        for from_xl in range(2):
            index = q * 2 + from_xl
            rows = out_ref.at[pl.ds((from_xl * 2 + (1 - core)) * SLAB + q * SHARE, SHARE)]
            remote(rows, rows, cs.at[index], cr.at[index], sibling).wait_recv()
    for copy in started:
        copy.wait_send()
    for piece, slot, group in pieces:
        for to_xl in range(2):

            @pl.when(jnp.logical_not((group == rep) & (xl == to_xl)))
            def _():
                plane_copy(piece, slot, group, to_xl).wait_send()


def gather_features(features):
    return pl.pallas_call(
        gather_kernel,
        out_shape=jax.ShapeDtypeStruct((SECTIONS * SLAB, F), BF16),
        in_specs=[VMEM],
        out_specs=VMEM,
        scratch_shapes=[
            pltpu.VMEM((8, SHARE, F), BF16),
            DMA((8,)),
            DMA((8,)),
            DMA((16,)),
            DMA((16,)),
            DMA((16,)),
            DMA((16,)),
        ],
        compiler_params=pltpu.CompilerParams(
            collective_id=0, has_side_effects=True, vmem_limit_bytes=32 * 1024 * 1024
        ),
        name="gather_features",
    )(features)


UNROLL = 4


def forward_kernel(rows, cols, counts, adj, source, out, total):
    total[...] = jnp.zeros_like(total)
    for section in range(SECTIONS):
        live = counts[0, section]

        def group(g, carry):
            products = []
            for u in range(UNROLL):
                slot = g * UNROLL + u
                first = pl.multiple_of(section * SLAB + cols[0, section, slot] * TILE, TILE)
                products.append(
                    jnp.dot(adj[section * CAP + slot], source[pl.ds(first, TILE), :], preferred_element_type=F32)
                )
            for u in range(UNROLL):
                slot = g * UNROLL + u
                put = pl.ds(pl.multiple_of(rows[0, section, slot] * TILE, TILE), TILE)
                total[put, :] += jnp.where(slot < live, products[u], 0.0)
            return carry

        lax.fori_loop(0, (live + UNROLL - 1) // UNROLL, group, 0)
    out[...] = total[...].astype(BF16)


def forward_tiles(rows, cols, counts, adj, source):
    return pl.pallas_call(
        forward_kernel,
        out_shape=jax.ShapeDtypeStruct((SLAB, F), BF16),
        in_specs=[SMEM, SMEM, SMEM, VMEM, VMEM],
        out_specs=VMEM,
        scratch_shapes=[pltpu.VMEM((SLAB, F), F32)],
        compiler_params=pltpu.CompilerParams(vmem_limit_bytes=32 * 1024 * 1024),
        name="forward_tiles",
    )(rows, cols, counts, adj, source)


def dense_kernel(
    part_ref, weight_ref, bias_ref, cot_ref, act_ref, back_ref, grad_ref, agg, inbox, wsum, bsum, s1, r1, s2, r2
):
    rep, blk, z, low, xl, core = place()
    peers = [(wrap(rep + k, REP), blk) for k in range(1, REP)]
    meet(peers)
    scatter = []
    for k in range(1, REP):
        to = wrap(rep + k, REP)
        copy = remote(part_ref.at[pl.ds(to * SHARE, SHARE)], inbox.at[k], s1.at[k], r1.at[k], (to, blk))
        copy.start()
        scatter.append(copy)
    own = pl.ds(pl.multiple_of(rep * SHARE, SHARE), SHARE)
    total = part_ref[own, :].astype(F32)
    for k in range(1, REP):
        scatter[k - 1].wait_recv()
        total += inbox[k].astype(F32)
    agg[own, :] = total.astype(BF16)
    gather = []
    for k in range(1, REP):
        to = wrap(rep + k, REP)
        copy = remote(agg.at[pl.ds(rep * SHARE, SHARE)], agg.at[pl.ds(rep * SHARE, SHARE)], s2.at[k], r2.at[k], (to, blk))
        copy.start()
        gather.append(copy)

    wsum[...] = jnp.zeros_like(wsum)
    bsum[...] = jnp.zeros_like(bsum)

    def dense(q):
        these = pl.ds(pl.multiple_of(q * SHARE, SHARE), SHARE)
        low_part = agg[these, :]
        pre = jnp.dot(low_part, weight_ref[...], preferred_element_type=F32) + bias_ref[...]
        s = jax.nn.sigmoid(pre)
        act_ref[these, :] = (pre * s).astype(BF16)
        grad = cot_ref[these, :].astype(F32) * s * (1.0 + pre * (1.0 - s))
        grad_low = grad.astype(BF16)
        bsum[...] += jnp.sum(grad.reshape(SHARE // 8, 8, H), axis=0)
        wsum[...] += lax.dot_general(low_part, grad_low, (((0,), (0,)), ((), ())), preferred_element_type=F32)
        turned = lax.dot_general(weight_ref[...], grad_low, (((1,), (1,)), ((), ())), preferred_element_type=F32)
        back_ref[2 * q] = turned[:, :TILE].astype(BF16)
        back_ref[2 * q + 1] = turned[:, TILE:].astype(BF16)

    dense(rep)
    for k in range(1, REP):
        q = wrap(rep - k, REP)
        remote(
            agg.at[pl.ds(rep * SHARE, SHARE)], agg.at[pl.ds(q * SHARE, SHARE)], s2.at[k], r2.at[k], (q, blk)
        ).wait_recv()
        dense(q)

    slab = wsum[pl.ds(pl.multiple_of(rep * 16, 16), 16), :]
    sums = bsum[...]
    for g in range(4):
        up, side = (g // 2) * 8, (g % 2) * 128
        grad_ref[g, 0:8, :] = slab[up : up + 8, side : side + 128]
        grad_ref[g, 8:16, :] = sums[:, 0:128]
        grad_ref[g, 16:24, :] = sums[:, 128:256]
    for copy in scatter + gather:
        copy.wait_send()


def dense_layer(partial, weight, bias, cotangent):
    return pl.pallas_call(
        dense_kernel,
        out_shape=(
            jax.ShapeDtypeStruct((SLAB, H), BF16),
            jax.ShapeDtypeStruct((PER_SIDE, F, TILE), BF16),
            jax.ShapeDtypeStruct((4, 24, 128), F32),
        ),
        in_specs=[VMEM] * 4,
        out_specs=(VMEM,) * 3,
        scratch_shapes=[
            pltpu.VMEM((SLAB, F), BF16),
            pltpu.VMEM((REP, SHARE, F), BF16),
            pltpu.VMEM((F, H), F32),
            pltpu.VMEM((8, H), F32),
            DMA((REP,)),
            DMA((REP,)),
            DMA((REP,)),
            DMA((REP,)),
        ],
        compiler_params=pltpu.CompilerParams(
            collective_id=1, has_side_effects=True, vmem_limit_bytes=32 * 1024 * 1024
        ),
        name="dense_layer",
    )(partial, weight, bias, cotangent)


def backward_kernel(rows, cols, counts, adj, back, out, total):
    for section in range(SECTIONS):
        total[...] = jnp.zeros_like(total)
        live = counts[0, section]

        def group(g, carry):
            products = []
            for u in range(UNROLL):
                slot = g * UNROLL + u
                products.append(
                    jnp.dot(back[rows[0, section, slot]], adj[section * CAP + slot], preferred_element_type=F32)
                )
            for u in range(UNROLL):
                slot = g * UNROLL + u
                put = cols[0, section, slot]
                total[put] += jnp.where(slot < live, products[u], 0.0)
            return carry

        lax.fori_loop(0, (live + UNROLL - 1) // UNROLL, group, 0)
        out[section * PER_SIDE : (section + 1) * PER_SIDE] = total[...].astype(BF16)


def backward_tiles(rows, cols, counts, adj, back):
    return pl.pallas_call(
        backward_kernel,
        out_shape=jax.ShapeDtypeStruct((SECTIONS * PER_SIDE, F, TILE), BF16),
        in_specs=[SMEM, SMEM, SMEM, VMEM, VMEM],
        out_specs=VMEM,
        scratch_shapes=[pltpu.VMEM((PER_SIDE, F, TILE), F32)],
        compiler_params=pltpu.CompilerParams(vmem_limit_bytes=32 * 1024 * 1024),
        name="backward_tiles",
    )(rows, cols, counts, adj, back)


ORDER = (4, 3, 5, 2, 6, 1, 7, 0)


def reduce_kernel(
    part_ref, grad_ref, out_ref, weight_ref, bias_ref,
    from_core, to_x, from_x, to_z, from_z, w1, w2own, w2, w3, w4,
    cs, cr, xs, xr, zs, zr, w1s, w1r, w2s, w2r, w3s, w3r, w4s, w4r,
):
    rep, blk, z, low, xl, core = place()
    sibling = (rep, z * 4 + xl * 2 + (1 - core))
    across = (rep, z * 4 + (1 - xl) * 2 + core)
    lows = [(rep, z * 4 + wrap(low + k, 4)) for k in range(1, 4)]
    zs_peers = [(rep, wrap(z + k, NZ) * 4 + low) for k in range(1, NZ)]
    reps = [(wrap(rep + k, REP), blk) for k in range(1, REP)]
    meet(lows + zs_peers + reps)
    started = []

    def start(copy):
        copy.start()
        started.append(copy)
        return copy

    core_copies = {}
    for k in ORDER:
        zt = wrap(z + k, NZ)
        core_copies[k] = [
            start(
                remote(
                    part_ref.at[pl.ds(2 * (zt * 4 + xt * 2 + (1 - core)), 2)],
                    from_core.at[k, xt],
                    cs.at[k, xt],
                    cr.at[k, xt],
                    sibling,
                )
            )
            for xt in range(2)
        ]
    w1_copies = [
        start(remote(grad_ref.at[wrap(low + k, 4)], w1.at[k], w1s.at[k], w1r.at[k], lows[k - 1])) for k in range(1, 4)
    ]

    x_copies = {}
    for k in ORDER:
        zt = wrap(z + k, NZ)
        for copy in core_copies[k]:
            copy.wait_recv()
        mine = part_ref[pl.ds(2 * (zt * 4 + (1 - xl) * 2 + core), 2)].astype(F32)
        to_x[k] = (mine + from_core[k, 1 - xl].astype(F32)).astype(BF16)
        x_copies[k] = start(remote(to_x.at[k], from_x.at[k], xs.at[k], xr.at[k], across))

    for copy in w1_copies:
        copy.wait_recv()
    w2own[...] = grad_ref[low] + w1[1] + w1[2] + w1[3]
    w2_copies = [
        start(remote(w2own, w2.at[k], w2s.at[k], w2r.at[k], zs_peers[k - 1])) for k in range(1, NZ)
    ]

    w3_copies = []
    z_copies = {}
    mine_last = None
    for k in ORDER:
        zt = wrap(z + k, NZ)
        x_copies[k].wait_recv()
        total = (
            part_ref[pl.ds(2 * (zt * 4 + xl * 2 + core), 2)].astype(F32)
            + from_core[k, xl].astype(F32)
            + from_x[k].astype(F32)
        )
        if k == 0:
            mine_last = total
        else:
            to_z[k] = total.astype(BF16)
            z_copies[k] = start(remote(to_z.at[k], from_z.at[k], zs.at[k], zr.at[k], zs_peers[k - 1]))
        if k == 3:
            summed = w2own[...]
            for j, copy in enumerate(w2_copies):
                copy.wait_recv()
                summed += w2[j + 1]
            w3[rep] = summed[0:8]
            bias_ref[:, 0:128] = jnp.sum(summed[8:16], axis=0, keepdims=True)
            bias_ref[:, 128:256] = jnp.sum(summed[16:24], axis=0, keepdims=True)
            w3_copies = [
                start(remote(w3.at[rep], w3.at[rep], w3s.at[j], w3r.at[j], reps[j - 1])) for j in range(1, REP)
            ]
        if k == 1:
            for j in range(1, REP):
                q = wrap(rep - j, REP)
                remote(w3.at[rep], w3.at[q], w3s.at[j], w3r.at[j], reps[j - 1]).wait_recv()
            for j in range(1, 4):
                start(remote(w3, w4.at[j], w4s.at[j], w4r.at[j], lows[j - 1]))
    total = mine_last
    for k in ORDER:
        if k:
            z_copies[k].wait_recv()
            total += from_z[k].astype(F32)
    out_ref[0:TILE, :] = total[0].T
    out_ref[TILE : 2 * TILE, :] = total[1].T

    def put(which, source):
        up, side = which // 2, lax.rem(which, 2)
        for q in range(REP):
            for s in range(2):

                @pl.when(side == s)
                def _():
                    weight_ref[pl.ds(pl.multiple_of(q * 16 + up * 8, 8), 8), s * 128 : (s + 1) * 128] = source[q]

    put(low, w3)
    for j in range(1, 4):
        remote(w3, w4.at[j], w4s.at[j], w4r.at[j], lows[j - 1]).wait_recv()
        put(wrap(low - j, 4), w4.at[j])
    for copy in started:
        copy.wait_send()


def reduce_blocks(parts, grads):
    pair = (2, F, TILE)
    return pl.pallas_call(
        reduce_kernel,
        out_shape=(
            jax.ShapeDtypeStruct((SHARE, F), F32),
            jax.ShapeDtypeStruct((F, H), F32),
            jax.ShapeDtypeStruct((1, H), F32),
        ),
        in_specs=[VMEM] * 2,
        out_specs=(VMEM,) * 3,
        scratch_shapes=[
            pltpu.VMEM((NZ, 2) + pair, BF16),
            pltpu.VMEM((NZ,) + pair, BF16),
            pltpu.VMEM((NZ,) + pair, BF16),
            pltpu.VMEM((NZ,) + pair, BF16),
            pltpu.VMEM((NZ,) + pair, BF16),
            pltpu.VMEM((4, 24, 128), F32),
            pltpu.VMEM((24, 128), F32),
            pltpu.VMEM((NZ, 24, 128), F32),
            pltpu.VMEM((REP, 8, 128), F32),
            pltpu.VMEM((4, REP, 8, 128), F32),
            DMA((NZ, 2)),
            DMA((NZ, 2)),
            DMA((NZ,)),
            DMA((NZ,)),
            DMA((NZ,)),
            DMA((NZ,)),
            DMA((4,)),
            DMA((4,)),
            DMA((NZ,)),
            DMA((NZ,)),
            DMA((REP,)),
            DMA((REP,)),
            DMA((4,)),
            DMA((4,)),
        ],
        compiler_params=pltpu.CompilerParams(
            collective_id=2, has_side_effects=True, vmem_limit_bytes=32 * 1024 * 1024
        ),
        name="reduce_blocks",
    )(parts, grads)


def on_device(features, weight, bias_vector, adj_tiles, tile_rows, tile_cols, counts, cotangent):
    adj = adj_tiles.reshape(SECTIONS * CAP, TILE, TILE)
    gathered = gather_features(features)
    partial = forward_tiles(tile_rows, tile_cols, counts, adj, gathered)
    activations, back, grads = dense_layer(partial, weight, bias_vector.reshape(1, H), cotangent)
    parts = backward_tiles(tile_rows, tile_cols, counts, adj, back)
    feature_grad, weight_grad, bias_grad = reduce_blocks(parts, grads)
    return activations, feature_grad, weight_grad, bias_grad.reshape(H)


def solution(mesh):
    placed = (
        P(("blk", "rep"), None),
        P(),
        P(),
        P("blk", "rep", None, None, None),
        P("blk", "rep", None),
        P("blk", "rep", None),
        P("blk", "rep"),
        P("blk", None),
    )
    return jax.shard_map(
        on_device,
        mesh=mesh,
        in_specs=placed,
        out_specs=(P("blk", None), P(("rep", "blk"), None), P(), P()),
        check_vma=False,
    )
```

time: 647 us -> 92.6 us (0.14)
  waiting for transfers between devices: 351 us -> 0 us
  blocking collectives: 197 us -> 0 us
  Pallas kernels: 0 us -> 87.9 us
  other arithmetic: 31 us -> 0 us
  local copies, waits for them, and re-layouts: 25.8 us -> 3.86 us
  matrix products: 16.8 us -> 0 us
  between operations: 13.8 us -> 0.77 us
  loops' own time: 8.21 us -> 0 us
    psum x2 -> x0, blocking collectives: 163 us -> none  [the longest x1 86.7 us: on_device(): weight_grad, bias_grad = lax.psum((weight_part, bias_part), ('rep', 'blk'))]
    psum x1 -> x0, waiting for transfers between devices: 122 us -> none  [on_device(): weight_grad, bias_grad = lax.psum((weight_part, bias_part), ('rep', 'blk'))]
    reduce_scatter x1 -> x0, waiting for transfers between devices: 120 us -> none  [on_device(): lax.psum_scatter(section_parts.reshape(sections * slab_rows, feat_width),...]
    all_gather x1 -> x0, waiting for transfers between devices: 108 us -> none  [on_device(): everything = lax.all_gather(own_panel, 'blk', axis=0, tiled=True)]
    pallas_call x0 -> x5, Pallas kernels: none -> 87.9 us  [the longest x1 31.8 us: gather_features(): pl.pallas_call(gather_kernel, out_shape=jax.ShapeDtypeStruct((SECTIONS *...]
    all_gather x1 -> x0, blocking collectives: 34 us -> none  [on_device(): own_panel = lax.all_gather(features, 'rep', axis=0, tiled=True)]
    dot_general x11 -> x0, matrix products: 16.8 us -> none  [the longest x4 5.71 us: slot_products(): jnp.einsum('cij,cif->cjf', tile_part, picked, preferred_element_type=jnp....]
    dynamic_slice x16 -> x0, local copies, waits for them, and re-layouts: 14 us -> none  [the longest x4 4.97 us: forward_terms(): counts[0, section]]
  transfers between devices with their start and end apart: 3 -> 0, of which waited for: 3 -> 0; matrix products, arithmetic and copies ran while one was open for 5% -> 0% of each run, Pallas kernels for 0% -> 0%
where the time goes in v1:
time: 92.6 us; the launch traced here: 92.5 us
  Pallas kernels  87.9 us (95%)
  local copies, waits for them, and re-layouts  3.86 us (4%)
    pallas_call x1, Pallas kernels, gather_features(): pl.pallas_call(gather_kernel, out_shape=jax.ShapeDtypeStruct((SECTIONS *...  31.8 us
    pallas_call x1, Pallas kernels, reduce_blocks(): pl.pallas_call(reduce_kernel, out_shape=(jax.ShapeDtypeStruct((SHARE, F),...  28 us
    pallas_call x1, Pallas kernels, dense_layer(): pl.pallas_call(dense_kernel, out_shape=(jax.ShapeDtypeStruct((SLAB, H), B...  24.4 us
    unnamed x20, local copies, waits for them, and re-layouts  3.86 us
    pallas_call x1, Pallas kernels, backward_tiles(): pl.pallas_call(backward_kernel, out_shape=jax.ShapeDtypeStruct((SECTIONS...  1.94 us

profile of v1, /device:TPU:1, one launch (start us, length us, event | category | flops | bytes accessed | tf_op | source)
XLA Modules:
  0.0 92.5 jit_solution(16653245729361304551)
XLA Ops:
  0.6 0.0 copy-start
  0.6 0.0 copy-start.2
  0.7 1.0 %copy-done.2 = bf16[256,128]{1,0:T(8,128)(2,1)S(1)} copy-done((bf16[256,128]{1,0:T(8,128)(2,1)S(1)}, bf16[256,128]{1,0:T(8,128)(2,1)}, u32[]{:S(2)}) %copy-start.2) | copy-done | bytes 65560
  1.6 0.0 copy-start.4
  1.6 0.0 copy-start.5
  1.6 0.0 copy-start.6
  1.6 31.8 %gather_features.1.source = bf16[8192,128]{1,0:T(8,128)(2,1)S(1)} custom-call(bf16[256,128]{1,0:T(8,128)(2,1)S(1)} %copy-done.2), custom_call_target="tpu_custom_call" | custom-call | tf_op jit(solution)/shard_map/gather_features/pallas_call | solution.py:150
  33.5 0.0 copy-done
  33.5 0.0 copy-done.4
  33.5 0.0 copy-done.5
  33.5 0.0 copy-done.6
  33.5 0.0 copy-start.1
  33.5 0.0 copy-start.3
  33.5 0.0 copy-start.7
  33.5 1.7 %forward_tiles.1.part_ref = bf16[2048,128]{1,0:T(8,128)(2,1)S(1)} custom-call(s32[1,4,16]{2,1,0:T(4,128)S(1)} %copy-done.4, s32[1,4,16]{2,1,0:T(4,128)S(1)} %copy-done.5, s32[1,4]{1,0:T(1,128)S(1)} %copy-done.6, bf16[64,128,128]{2,1,0:T(8,128)(2,1)S(1)} %bitcast.3, bf16[8192,128]{1,0:T(8,128)(2,1)S(1)} %gather_features.1.source), custom_call_target="tpu_custom_call" | custom-call | tf_op jit(solution)/shard_map/forward_tiles/pallas_call | solution.py:198
  35.3 0.0 copy-done.1
  35.3 0.0 copy-done.3
  35.3 0.0 copy-done.7
  35.3 24.4 %dense_layer.1 = (bf16[2048,256]{1,0:T(8,128)(2,1)S(1)}, bf16[16,128,128]{2,1,0:T(8,128)(2,1)S(1)}, f32[4,24,128]{2,1,0:T(8,128)S(1)}) custom-call(bf16[2048,128]{1,0:T(8,128)(2,1)S(1)} %forward_tiles.1.part_ref, bf16[128,256]{1,0:T(8,128)(2,1)S(1)} %copy-done.3, f32[1,256]{1,0:T(1,128)S(1)} %bitcast.6, bf16[2048,256]{1,0:T(8,128)(2,1)S(1)} %copy-done.1), custom_call_target="tpu_custom_call" | custom-call | tf_op jit(solution)/shard_map/dense_layer/pallas_call | solution.py:271
  59.7 1.9 %backward_tiles.1.part_ref = bf16[64,128,128]{2,1,0:T(8,128)(2,1)S(1)} custom-call(s32[1,4,16]{2,1,0:T(4,128)S(1)} %copy-done.4, s32[1,4,16]{2,1,0:T(4,128)S(1)} %copy-done.5, s32[1,4]{1,0:T(1,128)S(1)} %copy-done.6, bf16[64,128,128]{2,1,0:T(8,128)(2,1)S(1)} %bitcast.4, bf16[16,128,128]{2,1,0:T(8,128)(2,1)S(1)} %get-tuple-element.11.back), custom_call_target="tpu_custom_call" | custom-call | tf_op jit(solution)/shard_map/backward_tiles/pallas_call | solution.py:320
  61.7 28.0 %reduce_blocks.1 = (f32[256,128]{1,0:T(8,128)S(1)}, f32[128,256]{1,0:T(8,128)S(1)}, f32[1,256]{1,0:T(1,128)S(1)}) custom-call(bf16[64,128,128]{2,1,0:T(8,128)(2,1)S(1)} %backward_tiles.1.part_ref, f32[4,24,128]{2,1,0:T(8,128)S(1)} %get-tuple-element.12.grad_ref), custom_call_target="tpu_custom_call" | custom-call | tf_op jit(solution)/shard_map/reduce_blocks/pallas_call | solution.py:448
  89.7 1.0 %copy.16 = bf16[2048,256]{1,0:T(8,128)(2,1)} copy(bf16[2048,256]{1,0:T(8,128)(2,1)S(1)} %get-tuple-element.20) | data formatting | bytes 2097152
  90.6 0.7 copy.17
  91.3 0.7 copy.18
  92.0 0.6 copy.19
Async XLA Ops:
  0.6 32.8 %copy-start = (bf16[1,4,16,128,128]{4,3,2,1,0:T(8,128)(2,1)S(1)}, bf16[1,4,16,128,128]{4,3,2,1,0:T(8,128)(2,1)}, u32[]{:S(2)}) copy-start(bf16[1,4,16,128,128]{4,3,2,1,0:T(8,128)(2,1)} %param.11) | copy-start | bytes 6291460
  0.6 1.0 %copy-start.2 = (bf16[256,128]{1,0:T(8,128)(2,1)S(1)}, bf16[256,128]{1,0:T(8,128)(2,1)}, u32[]{:S(2)}) copy-start(bf16[256,128]{1,0:T(8,128)(2,1)} %own_ref.1) | copy-start | bytes 196612
  1.6 31.9 %copy-start.4 = (s32[1,4,16]{2,1,0:T(4,128)S(1)}, s32[1,4,16]{2,1,0:T(4,128)}, u32[]{:S(2)}) copy-start(s32[1,4,16]{2,1,0:T(4,128)} %rows.3) | copy-start | bytes 772
  1.6 31.9 %copy-start.5 = (s32[1,4,16]{2,1,0:T(4,128)S(1)}, s32[1,4,16]{2,1,0:T(4,128)}, u32[]{:S(2)}) copy-start(s32[1,4,16]{2,1,0:T(4,128)} %cols.3) | copy-start | bytes 772
  1.6 31.9 %copy-start.6 = (s32[1,4]{1,0:T(1,128)S(1)}, s32[1,4]{1,0:T(1,128)}, u32[]{:S(2)}) copy-start(s32[1,4]{1,0:T(1,128)} %counts.3) | copy-start | bytes 52
  33.5 1.7 %copy-start.1 = (bf16[2048,256]{1,0:T(8,128)(2,1)S(1)}, bf16[2048,256]{1,0:T(8,128)(2,1)}, u32[]{:S(2)}) copy-start(bf16[2048,256]{1,0:T(8,128)(2,1)} %cot_ref.1) | copy-start | bytes 3145732
  33.5 1.7 %copy-start.3 = (bf16[128,256]{1,0:T(8,128)(2,1)S(1)}, bf16[128,256]{1,0:T(8,128)(2,1)}, u32[]{:S(2)}) copy-start(bf16[128,256]{1,0:T(8,128)(2,1)} %weight_ref.1) | copy-start | bytes 196612
  33.5 1.7 %copy-start.7 = (f32[256]{0:T(256)S(1)}, f32[256]{0:T(256)}, u32[]{:S(2)}) copy-start(f32[256]{0:T(256)} %param.10) | copy-start | bytes 3076

commit v2 on v0

v2 whole, which is shorter than its diff:
```python
import jax
import jax.numpy as jnp
from jax import lax
from jax.experimental import pallas as pl
from jax.experimental.pallas import tpu as pltpu
from jax.sharding import PartitionSpec as P

MESH = pl.DeviceIdType.MESH
F32 = jnp.float32
BF16 = jnp.bfloat16
HBM = pl.BlockSpec(memory_space=pltpu.HBM)
DMA = pltpu.SemaphoreType.DMA

REP = 8
BLK = 32
NZ = 8
SECTIONS = 4
CAP = 16
TILE = 128
PER_SIDE = 16
SLAB = 2048
SHARE = 256
F = 128
H = 256


def remote(src, dst, send_sem, recv_sem, device):
    return pltpu.make_async_remote_copy(
        src_ref=src,
        dst_ref=dst,
        send_sem=send_sem,
        recv_sem=recv_sem,
        device_id=device,
        device_id_type=MESH,
    )


def meet(peers):
    barrier = pltpu.get_barrier_semaphore()
    for peer in peers:
        pl.semaphore_signal(barrier, inc=1, device_id=peer, device_id_type=MESH)
    pl.semaphore_wait(barrier, len(peers))


def wrap(value, size):
    return lax.rem(value + size, size)


def place():
    rep = lax.axis_index("rep")
    blk = lax.axis_index("blk")
    z = blk // 4
    low = lax.rem(blk, 4)
    return rep, blk, z, low, low // 2, lax.rem(low, 2)


PLANE = ((2, 1), (1, 1), (3, 1), (2, 0), (0, 1), (1, 0), (3, 0))
SECTION_ORDER = (2, 1, 3, 0)
SLOTS = SECTIONS * CAP
UNROLL = 4


def layer_kernel(
    own_hbm, weight_hbm, bias_hbm, rows_hbm, cols_hbm, counts_hbm, adj_hbm, cot_hbm,
    act_hbm, feature_hbm, wgrad_hbm, bgrad_hbm,
    weight_ref, bias_ref, rows_ref, cols_ref, counts_ref, adj, cot, act_ref, feature_ref, wgrad_ref, bgrad_ref, ring, here, there, sums, plan_v, plan,
    to_rep, inbox, agg, back, wsum, bsum, grads,
    to_core, from_core, to_x, from_x, to_z, from_z, w1, w2own, w2, w3, w4,
    ls, os, zs, zr, ps, pr, cs, cr, s1, r1, s2, r2,
    ds, dr, xs, xr, es, er, w1s, w1r, w2s, w2r, w3s, w3r, w4s, w4r,
):
    rep, blk, z, low, xl, core = place()
    y, xh = rep // 2, lax.rem(rep, 2)

    def at_z(step):
        return (rep, wrap(z + step, NZ) * 4 + low)

    sibling = (rep, z * 4 + xl * 2 + (1 - core))
    across = (rep, z * 4 + (1 - xl) * 2 + core)
    lows = [(rep, z * 4 + wrap(low + k, 4)) for k in range(1, 4)]
    ahead = [lax.rem(y + dy, 4) * 2 + lax.rem(xh + dx, 2) for dy, dx in PLANE]
    behind = [lax.rem(y + 4 - dy, 4) * 2 + lax.rem(xh + dx, 2) for dy, dx in PLANE]

    own_ref = ring.at[0]

    def load(n, source, target):
        copy = pltpu.make_async_copy(source, target, ls.at[n])
        copy.start()
        return copy

    load_own = load(0, own_hbm, own_ref)
    load_lists = [load(1, rows_hbm, rows_ref), load(2, cols_hbm, cols_ref), load(3, counts_hbm, counts_ref)]
    load_adj = load(4, adj_hbm, adj)
    load_dense = [load(5, cot_hbm, cot), load(6, weight_hbm, weight_ref), load(7, bias_hbm, bias_ref)]

    peers = [at_z(k) for k in range(1, NZ)] + lows
    peers += [(q, z * 4 + x * 2 + core) for q in ahead for x in range(2)]
    meet(peers)

    started = []

    def start(copy):
        copy.start()
        started.append(copy)
        return copy


    def along_z(source, slot, step):
        return remote(source, ring.at[slot], zs.at[slot], zr.at[slot], at_z(step))

    load_own.wait()
    start(along_z(own_ref, 2, 2))
    start(along_z(own_ref, 6, -2))
    start(along_z(own_ref, 1, 1))
    start(along_z(own_ref, 7, -1))

    def in_plane(piece, slot, group, to_xl):
        return remote(
            piece,
            here.at[pl.ds(xl * PER_SIDE + rep * 2, 2)],
            ps.at[slot * 2 + to_xl],
            pr.at[rep * 2 + xl],
            (group, z * 4 + to_xl * 2 + core),
        )

    pieces = []

    def spread(piece, slot):
        group = wrap(z - slot, NZ)
        pieces.append((piece, slot, group))
        for to_xl in range(2):
            mine = (group == rep) & (xl == to_xl)

            @pl.when(mine)
            def _():
                here[pl.ds(xl * PER_SIDE + rep * 2, 2)] = piece[...]

            @pl.when(jnp.logical_not(mine))
            def _():
                in_plane(piece, slot, group, to_xl).start()

    spread(own_ref, 0)

    for copy in load_lists:
        copy.wait()
    lane = lax.broadcasted_iota(jnp.int32, (1, 128), 1)
    none = jnp.full((1, 128), -1, jnp.int32)
    zero_tile = jnp.full((1, 128), SLOTS, jnp.int32)

    def forward_section(turn):
        return lax.rem(turn, 2) * 2 + lax.rem(core + turn // 2, 2)

    def keys(c):
        section, slot = c // CAP, lax.rem(c, CAP)
        col_key = jnp.where(slot < counts_ref[0, section], cols_ref[0, section, slot] + section * PER_SIDE, -1)
        section = forward_section(section)
        row_key = jnp.where(slot < counts_ref[0, section], rows_ref[0, section, slot], -1)
        return row_key, col_key

    def spell(c, carry):
        row_key, col_key = keys(c)
        return jnp.where(lane == c, row_key, carry[0]), jnp.where(lane == c, col_key, carry[1])

    row_keys, col_keys = lax.fori_loop(0, SLOTS, spell, (none, none))

    def chain(c, carry):
        row_key, col_key = keys(c)
        row_prev, row_last, col_prev, col_last = carry
        later = lane > c
        return (
            jnp.where((row_keys == row_key) & later, c, row_prev),
            jnp.where(lane == row_key, c, row_last),
            jnp.where((col_keys == col_key) & later, c, col_prev),
            jnp.where(lane == col_key, c, col_last),
        )

    tables = lax.fori_loop(0, SLOTS, chain, (zero_tile,) * 4)
    for i in range(4):
        plan_v[i : i + 1, :] = tables[i]
    load_plan = load(8, plan_v, plan)

    def arrive(slot):
        along_z(own_ref, slot, 1).wait_recv()

    arrive(2)
    start(along_z(ring.at[2], 3, 1))
    arrive(6)
    start(along_z(ring.at[6], 5, -1))
    start(along_z(ring.at[2 + 4 * core], 4, 2 - 4 * core))
    spread(ring.at[2], 2)
    spread(ring.at[6], 6)
    for slot in (1, 7, 3, 5, 4):
        arrive(slot)
        spread(ring.at[slot], slot)

    for q in [rep] + behind:
        for x in range(2):
            index = q * 2 + x
            tiles = pl.ds(x * PER_SIDE + q * 2, 2)
            arrival = remote(own_ref, here.at[tiles], ps.at[0], pr.at[index], sibling)
            if q is rep:

                @pl.when(xl != x)
                def _():
                    arrival.wait_recv()
            else:
                arrival.wait_recv()
            start(remote(here.at[tiles], there.at[tiles], cs.at[index], cr.at[index], sibling))


    load_plan.wait()
    load_adj.wait()
    sums[SLOTS] = jnp.zeros((TILE, F), F32)

    def forward(source, turn):
        section = forward_section(turn)

        def group(g, carry):
            products = []
            for u in range(UNROLL):
                slot = g * UNROLL + u
                products.append(
                    jnp.dot(
                        adj[section * CAP + slot],
                        source[lax.rem(turn, 2) * PER_SIDE + cols_ref[0, section, slot]],
                        preferred_element_type=F32,
                    )
                )
            for u in range(UNROLL):
                c = turn * CAP + g * UNROLL + u
                sums[c] = products[u] + sums[plan[0, c]]
            return carry

        lax.fori_loop(0, CAP // UNROLL, group, 0)

    for turn in range(2):
        forward(here, turn)
    for q in [rep] + behind:
        for x in range(2):
            index = q * 2 + x
            tiles = pl.ds(x * PER_SIDE + q * 2, 2)
            remote(here.at[tiles], there.at[tiles], cs.at[index], cr.at[index], sibling).wait_recv()
    for turn in range(2, 4):
        forward(there, turn)

    scatter = []
    for m, q in enumerate(ahead):
        to_rep[m, 0] = sums[plan[1, 2 * q]].astype(BF16)
        to_rep[m, 1] = sums[plan[1, 2 * q + 1]].astype(BF16)
        scatter.append(start(remote(to_rep.at[m], inbox.at[m], s1.at[m], r1.at[m], (q, blk))))
    first = sums[plan[1, 2 * rep]]
    second = sums[plan[1, 2 * rep + 1]]
    for m in range(REP - 1):
        scatter[m].wait_recv()
        first += inbox[m, 0].astype(F32)
        second += inbox[m, 1].astype(F32)
    agg[2 * rep] = first.astype(BF16)
    agg[2 * rep + 1] = second.astype(BF16)
    own = agg.at[pl.ds(2 * rep, 2)]
    for m, q in enumerate(ahead):
        start(remote(own, own, s2.at[m], r2.at[m], (q, blk)))


    wsum[...] = jnp.zeros_like(wsum)
    bsum[...] = jnp.zeros_like(bsum)
    for copy in load_dense:
        copy.wait()
    stores = []

    def store_part(n, source, target):
        copy = pltpu.make_async_copy(source, target, os.at[n])
        copy.start()
        stores.append(copy)

    def dense(q):
        these = pl.ds(pl.multiple_of(q * SHARE, SHARE), SHARE)
        low_part = agg[pl.ds(2 * q, 2)].reshape(SHARE, F)
        pre = jnp.dot(low_part, weight_ref[...], preferred_element_type=F32) + bias_ref[...]
        s = jax.nn.sigmoid(pre)
        act_ref[these, :] = (pre * s).astype(BF16)
        grad = cot[these, :].astype(F32) * s * (1.0 + pre * (1.0 - s))
        grad_low = grad.astype(BF16)
        bsum[...] += jnp.sum(grad.reshape(SHARE // 8, 8, H), axis=0)
        wsum[...] += lax.dot_general(low_part, grad_low, (((0,), (0,)), ((), ())), preferred_element_type=F32)
        turned = lax.dot_general(weight_ref[...], grad_low, (((1,), (1,)), ((), ())), preferred_element_type=F32)
        back[2 * q] = turned[:, :TILE].astype(BF16)
        back[2 * q + 1] = turned[:, TILE:].astype(BF16)
        store_part(len(stores), act_ref.at[pl.ds(q * SHARE, SHARE)], act_hbm.at[pl.ds(q * SHARE, SHARE)])

    dense(rep)
    for m, q in enumerate(behind):
        remote(own, agg.at[pl.ds(2 * q, 2)], s2.at[m], r2.at[m], (q, blk)).wait_recv()
        dense(q)


    slab = wsum[pl.ds(pl.multiple_of(rep * 16, 16), 16), :]
    partial_bias = bsum[...]
    for g in range(4):
        up, side = (g // 2) * 8, (g % 2) * 128
        grads[g, 0:8, :] = slab[up : up + 8, side : side + 128]
        grads[g, 8:16, :] = partial_bias[:, 0:128]
        grads[g, 16:24, :] = partial_bias[:, 128:256]
    w1_copies = [
        start(remote(grads.at[wrap(low + k, 4)], w1.at[k], w1s.at[k], w1r.at[k], lows[k - 1])) for k in range(1, 4)
    ]


    flip = lax.rem(z, 2)
    halves = []
    for j, step in enumerate(SECTION_ORDER):
        section = lax.rem(z // 2 + step, 4)
        halves.append([section * 2 + (1 - flip), section * 2 + flip])

    def sum_of(zt, x, c):
        tile = 2 * (zt * 4 + x * 2 + c)
        return sums[plan[3, tile]], sums[plan[3, tile + 1]]

    w2_copies = []
    core_copies = {}
    x_copies = {}

    def send_across(j):
        for h in range(2):
            core_copies[j, h].wait_recv()
            a, b = sum_of(halves[j][h], 1 - xl, core)
            to_x[j, h, 0] = (a + from_core[j, h, 1 - xl, 0].astype(F32)).astype(BF16)
            to_x[j, h, 1] = (b + from_core[j, h, 1 - xl, 1].astype(F32)).astype(BF16)
            x_copies[j, h] = start(
                remote(to_x.at[j, h], from_x.at[j, h], xs.at[j, h], xr.at[j, h], across)
            )

    for j, step in enumerate(SECTION_ORDER):
        section = lax.rem(z // 2 + step, 4)

        def group(g, carry):
            products = []
            for u in range(UNROLL):
                slot = g * UNROLL + u
                products.append(
                    jnp.dot(back[rows_ref[0, section, slot]], adj[section * CAP + slot], preferred_element_type=F32)
                )
            for u in range(UNROLL):
                c = section * CAP + g * UNROLL + u
                sums[c] = products[u] + sums[plan[2, c]]
            return carry

        lax.fori_loop(0, CAP // UNROLL, group, 0)
        for h in range(2):
            for x in range(2):
                a, b = sum_of(halves[j][h], x, 1 - core)
                to_core[j, h, x, 0] = a.astype(BF16)
                to_core[j, h, x, 1] = b.astype(BF16)
            core_copies[j, h] = start(
                remote(to_core.at[j, h], from_core.at[j, h], ds.at[j, h], dr.at[j, h], sibling)
            )
        if j == 0:
            for copy in w1_copies:
                copy.wait_recv()
            w2own[...] = grads[low] + w1[1] + w1[2] + w1[3]
            w2_copies = [
                start(remote(w2own, w2.at[k], w2s.at[k], w2r.at[k], at_z(k))) for k in range(1, NZ)
            ]
        if j:
            send_across(j - 1)
    send_across(3)

    summed = w2own[...]
    for i, copy in enumerate(w2_copies):
        copy.wait_recv()
        summed += w2[i + 1]
    w3[rep] = summed[0:8]
    bgrad_ref[:, 0:128] = jnp.sum(summed[8:16], axis=0, keepdims=True)
    bgrad_ref[:, 128:256] = jnp.sum(summed[16:24], axis=0, keepdims=True)
    for m, q in enumerate(ahead):
        start(remote(w3.at[rep], w3.at[rep], w3s.at[m], w3r.at[m], (q, blk)))

    z_copies = {}
    kept = None
    for j in range(4):
        for h in range(2):
            zt = halves[j][h]
            x_copies[j, h].wait_recv()
            a, b = sum_of(zt, xl, core)
            a = a + from_core[j, h, xl, 0].astype(F32) + from_x[j, h, 0].astype(F32)
            b = b + from_core[j, h, xl, 1].astype(F32) + from_x[j, h, 1].astype(F32)
            if (j, h) == (3, 1):
                kept = (a, b)
            else:
                k = wrap(zt - z, NZ)
                to_z[j, h, 0] = a.astype(BF16)
                to_z[j, h, 1] = b.astype(BF16)
                z_copies[j, h] = start(
                    remote(to_z.at[j, h], from_z.at[k], es.at[k], er.at[k], (rep, zt * 4 + low))
                )
        if j == 1:
            for m, q in enumerate(behind):
                remote(w3.at[rep], w3.at[q], w3s.at[m], w3r.at[m], (q, blk)).wait_recv()
            for i in range(1, 4):
                start(remote(w3, w4.at[i], w4s.at[i], w4r.at[i], lows[i - 1]))

    def put(which, source):
        up, side = which // 2, lax.rem(which, 2)
        for s in range(2):

            @pl.when(side == s)
            def _():
                for q in range(REP):
                    wgrad_ref[pl.ds(pl.multiple_of(q * 16 + up * 8, 8), 8), s * 128 : (s + 1) * 128] = source[q]

    put(low, w3)
    for i in range(1, 4):
        remote(w3, w4.at[i], w4s.at[i], w4r.at[i], lows[i - 1]).wait_recv()
        put(wrap(low - i, 4), w4.at[i])
    store_part(8, wgrad_ref, wgrad_hbm)
    store_part(9, bgrad_ref, bgrad_hbm)

    a, b = kept
    for k in (4, 3, 5, 2, 6, 1, 7):
        remote(to_z.at[0, 0], from_z.at[k], es.at[k], er.at[k], at_z(k)).wait_recv()
        a += from_z[k, 0].astype(F32)
        b += from_z[k, 1].astype(F32)
    feature_ref[0:TILE, :] = a.T
    feature_ref[TILE : 2 * TILE, :] = b.T
    store_part(10, feature_ref, feature_hbm)
    for copy in started:
        copy.wait_send()
    for piece, slot, group in pieces:
        for to_xl in range(2):

            @pl.when(jnp.logical_not((group == rep) & (xl == to_xl)))
            def _():
                in_plane(piece, slot, group, to_xl).wait_send()

    for copy in stores:
        copy.wait()


def layer(own, weight, bias, rows, cols, counts, adj, cotangent):
    tiles = (2, TILE, F)
    return pl.pallas_call(
        layer_kernel,
        out_shape=(
            jax.ShapeDtypeStruct((SLAB, H), BF16),
            jax.ShapeDtypeStruct((SHARE, F), F32),
            jax.ShapeDtypeStruct((F, H), F32),
            jax.ShapeDtypeStruct((1, H), F32),
        ),
        in_specs=[HBM] * 8,
        out_specs=(HBM,) * 4,
        scratch_shapes=[
            pltpu.VMEM((F, H), BF16),
            pltpu.VMEM((1, H), F32),
            pltpu.SMEM((1, SECTIONS, CAP), jnp.int32),
            pltpu.SMEM((1, SECTIONS, CAP), jnp.int32),
            pltpu.SMEM((1, SECTIONS), jnp.int32),
            pltpu.VMEM((SLOTS, TILE, TILE), BF16),
            pltpu.VMEM((SLAB, H), BF16),
            pltpu.VMEM((SLAB, H), BF16),
            pltpu.VMEM((SHARE, F), F32),
            pltpu.VMEM((F, H), F32),
            pltpu.VMEM((1, H), F32),
            pltpu.VMEM((NZ,) + tiles, BF16),
            pltpu.VMEM((2 * PER_SIDE, TILE, F), BF16),
            pltpu.VMEM((2 * PER_SIDE, TILE, F), BF16),
            pltpu.VMEM((SLOTS + 1, TILE, F), F32),
            pltpu.VMEM((8, 128), jnp.int32),
            pltpu.SMEM((8, 128), jnp.int32),
            pltpu.VMEM((REP - 1,) + tiles, BF16),
            pltpu.VMEM((REP - 1,) + tiles, BF16),
            pltpu.VMEM((PER_SIDE, TILE, F), BF16),
            pltpu.VMEM((PER_SIDE, F, TILE), BF16),
            pltpu.VMEM((F, H), F32),
            pltpu.VMEM((8, H), F32),
            pltpu.VMEM((4, 24, 128), F32),
            pltpu.VMEM((4, 2, 2) + tiles, BF16),
            pltpu.VMEM((4, 2, 2) + tiles, BF16),
            pltpu.VMEM((4, 2) + tiles, BF16),
            pltpu.VMEM((4, 2) + tiles, BF16),
            pltpu.VMEM((4, 2) + tiles, BF16),
            pltpu.VMEM((NZ,) + tiles, BF16),
            pltpu.VMEM((4, 24, 128), F32),
            pltpu.VMEM((24, 128), F32),
            pltpu.VMEM((NZ, 24, 128), F32),
            pltpu.VMEM((REP, 8, 128), F32),
            pltpu.VMEM((4, REP, 8, 128), F32),
            DMA((9,)),
            DMA((11,)),
            DMA((NZ,)),
            DMA((NZ,)),
            DMA((16,)),
            DMA((16,)),
            DMA((16,)),
            DMA((16,)),
            DMA((REP - 1,)),
            DMA((REP - 1,)),
            DMA((REP - 1,)),
            DMA((REP - 1,)),
            DMA((4, 2)),
            DMA((4, 2)),
            DMA((4, 2)),
            DMA((4, 2)),
            DMA((NZ,)),
            DMA((NZ,)),
            DMA((4,)),
            DMA((4,)),
            DMA((NZ,)),
            DMA((NZ,)),
            DMA((REP - 1,)),
            DMA((REP - 1,)),
            DMA((4,)),
            DMA((4,)),
        ],
        compiler_params=pltpu.CompilerParams(
            collective_id=0, has_side_effects=True, vmem_limit_bytes=62 * 1024 * 1024
        ),
        name="layer",
    )(own, weight, bias, rows, cols, counts, adj, cotangent)


def store_kernel(act_in, feature_in, wgrad_in, bgrad_in, act_out, feature_out, wgrad_out, bgrad_out, *scratch):
    act, feature, wgrad, bgrad, in_sems, out_sems = scratch
    parts = [
        (act_in.at[rows], act.at[rows], act_out.at[rows])
        for rows in (pl.ds(first, SLAB // 4) for first in range(0, SLAB, SLAB // 4))
    ]
    parts += [(feature_in, feature, feature_out), (wgrad_in, wgrad, wgrad_out), (bgrad_in, bgrad, bgrad_out)]
    loads = [pltpu.make_async_copy(a, b, in_sems.at[n]) for n, (a, b, _) in enumerate(parts)]
    stores = [pltpu.make_async_copy(b, c, out_sems.at[n]) for n, (_, b, c) in enumerate(parts)]
    for copy in loads:
        copy.start()
    for arrive, leave in zip(loads, stores):
        arrive.wait()
        leave.start()
    for copy in stores:
        copy.wait()


def store(*arrays):
    return pl.pallas_call(
        store_kernel,
        out_shape=tuple(jax.ShapeDtypeStruct(a.shape, a.dtype) for a in arrays),
        in_specs=[HBM] * 4,
        out_specs=(HBM,) * 4,
        scratch_shapes=[pltpu.VMEM(a.shape, a.dtype) for a in arrays] + [DMA((7,)), DMA((7,))],
        compiler_params=pltpu.CompilerParams(vmem_limit_bytes=62 * 1024 * 1024),
        name="store",
    )(*arrays)


def on_device(features, weight, bias_vector, adj_tiles, tile_rows, tile_cols, counts, cotangent):
    results = layer(
        features.reshape(2, TILE, F),
        weight,
        bias_vector.reshape(1, H),
        tile_rows,
        tile_cols,
        counts,
        adj_tiles.reshape(SLOTS, TILE, TILE),
        cotangent,
    )
    activations, feature_grad, weight_grad, bias_grad = store(*results)
    return activations, feature_grad, weight_grad, bias_grad.reshape(H)


def solution(mesh):
    placed = (
        P(("blk", "rep"), None),
        P(),
        P(),
        P("blk", "rep", None, None, None),
        P("blk", "rep", None),
        P("blk", "rep", None),
        P("blk", "rep"),
        P("blk", None),
    )
    return jax.shard_map(
        on_device,
        mesh=mesh,
        in_specs=placed,
        out_specs=(P("blk", None), P(("rep", "blk"), None), P(), P()),
        check_vma=False,
    )
```

time: 647 us -> 85.7 us (0.13)
  the two profiles are of different devices: /device:TPU:1 before, /device:TPU:32 now
where the time goes in v2:
time: 85.7 us; the launch traced here: 85.6 us
  Pallas kernels  84.9 us (99%)
    pallas_call x1, Pallas kernels, layer(): pl.pallas_call(layer_kernel, out_shape=(jax.ShapeDtypeStruct((SLAB, H), B...  82.8 us
    pallas_call x1, Pallas kernels, store(): pl.pallas_call(store_kernel, out_shape=tuple((jax.ShapeDtypeStruct(a.shap...  2.12 us

profile of v2, /device:TPU:32, one launch (start us, length us, event | category | flops | bytes accessed | tf_op | source)
XLA Modules:
  0.0 85.6 jit_solution(661464456394675090)
XLA Ops:
  0.6 82.8 %layer.1 = (bf16[2048,256]{1,0:T(8,128)(2,1)}, f32[256,128]{1,0:T(8,128)}, f32[128,256]{1,0:T(8,128)}, f32[1,256]{1,0:T(1,128)}) custom-call(bf16[2,128,128]{2,1,0:T(8,128)(2,1)} %bitcast.5, bf16[128,256]{1,0:T(8,128)(2,1)} %weight_hbm.1, f32[1,256]{1,0:T(1,128)} %bitcast.6, s32[1,4,16]{2,1,0:T(4,128)} %rows_hbm.1, s32[1,4,16]{2,1,0:T(4,128)} %cols_hbm.1, ...), custom_call_target="tpu_custom_call" | custom-call | tf_op jit(solution)/shard_map/layer/pallas_call | solution.py:440
  83.5 2.1 %store.1 = (bf16[2048,256]{1,0:T(8,128)(2,1)}, f32[256,128]{1,0:T(8,128)}, f32[128,256]{1,0:T(8,128)}, f32[1,256]{1,0:T(1,128)}) custom-call(bf16[2048,256]{1,0:T(8,128)(2,1)} %get-tuple-element.12.act_in, f32[256,128]{1,0:T(8,128)} %get-tuple-element.13.feature_in, f32[128,256]{1,0:T(8,128)} %get-tuple-element.14.wgrad_in, f32[1,256]{1,0:T(1,128)} %get-tuple-element.15.bgrad_in), custom_call_target="tpu_custom_call" | custom-call | tf_op jit(solution)/shard_map/store/pallas_call | solution.py:539

commit v3 on v2

--- a/solution.py
+++ b/solution.py
@@ -93,7 +93,7 @@
     load_adj = load(4, adj_hbm, adj)
     load_dense = [load(5, cot_hbm, cot), load(6, weight_hbm, weight_ref), load(7, bias_hbm, bias_ref)]
 
-    peers = [at_z(k) for k in range(1, NZ)] + lows
+    peers = [at_z(k) for k in (2, -2, 1, -1)] + lows
     peers += [(q, z * 4 + x * 2 + core) for q in ahead for x in range(2)]
     meet(peers)
 
@@ -193,7 +193,7 @@
         arrive(slot)
         spread(ring.at[slot], slot)
 
-    for q in [rep] + behind:
+    for q in [rep] + behind[::-1]:
         for x in range(2):
             index = q * 2 + x
             tiles = pl.ds(x * PER_SIDE + q * 2, 2)
@@ -243,22 +243,22 @@
     for turn in range(2, 4):
         forward(there, turn)
 
-    scatter = []
-    for m, q in enumerate(ahead):
-        to_rep[m, 0] = sums[plan[1, 2 * q]].astype(BF16)
-        to_rep[m, 1] = sums[plan[1, 2 * q + 1]].astype(BF16)
-        scatter.append(start(remote(to_rep.at[m], inbox.at[m], s1.at[m], r1.at[m], (q, blk))))
-    first = sums[plan[1, 2 * rep]]
-    second = sums[plan[1, 2 * rep + 1]]
-    for m in range(REP - 1):
-        scatter[m].wait_recv()
-        first += inbox[m, 0].astype(F32)
-        second += inbox[m, 1].astype(F32)
-    agg[2 * rep] = first.astype(BF16)
-    agg[2 * rep + 1] = second.astype(BF16)
-    own = agg.at[pl.ds(2 * rep, 2)]
-    for m, q in enumerate(ahead):
-        start(remote(own, own, s2.at[m], r2.at[m], (q, blk)))
+    scatter = {}
+    for half in range(2):
+        for m, q in enumerate(ahead):
+            to_rep[half, m] = sums[plan[1, 2 * q + half]].astype(BF16)
+            scatter[half, m] = start(
+                remote(to_rep.at[half, m], inbox.at[half, m], s1.at[half, m], r1.at[half, m], (q, blk))
+            )
+    for half in range(2):
+        total = sums[plan[1, 2 * rep + half]]
+        for m in range(REP - 1):
+            scatter[half, m].wait_recv()
+            total += inbox[half, m].astype(F32)
+        agg[2 * rep + half] = total.astype(BF16)
+        for m, q in enumerate(ahead):
+            own = agg.at[2 * rep + half]
+            start(remote(own, own, s2.at[half, m], r2.at[half, m], (q, blk)))
 
 
     wsum[...] = jnp.zeros_like(wsum)
@@ -272,25 +272,26 @@
         copy.start()
         stores.append(copy)
 
-    def dense(q):
-        these = pl.ds(pl.multiple_of(q * SHARE, SHARE), SHARE)
-        low_part = agg[pl.ds(2 * q, 2)].reshape(SHARE, F)
+    def dense(tile):
+        these = pl.ds(pl.multiple_of(tile * TILE, TILE), TILE)
+        low_part = agg[tile]
         pre = jnp.dot(low_part, weight_ref[...], preferred_element_type=F32) + bias_ref[...]
         s = jax.nn.sigmoid(pre)
         act_ref[these, :] = (pre * s).astype(BF16)
         grad = cot[these, :].astype(F32) * s * (1.0 + pre * (1.0 - s))
         grad_low = grad.astype(BF16)
-        bsum[...] += jnp.sum(grad.reshape(SHARE // 8, 8, H), axis=0)
+        bsum[...] += jnp.sum(grad.reshape(TILE // 8, 8, H), axis=0)
         wsum[...] += lax.dot_general(low_part, grad_low, (((0,), (0,)), ((), ())), preferred_element_type=F32)
         turned = lax.dot_general(weight_ref[...], grad_low, (((1,), (1,)), ((), ())), preferred_element_type=F32)
-        back[2 * q] = turned[:, :TILE].astype(BF16)
-        back[2 * q + 1] = turned[:, TILE:].astype(BF16)
-        store_part(len(stores), act_ref.at[pl.ds(q * SHARE, SHARE)], act_hbm.at[pl.ds(q * SHARE, SHARE)])
-
-    dense(rep)
-    for m, q in enumerate(behind):
-        remote(own, agg.at[pl.ds(2 * q, 2)], s2.at[m], r2.at[m], (q, blk)).wait_recv()
-        dense(q)
+        back[tile] = turned.astype(BF16)
+        store_part(len(stores), act_ref.at[pl.ds(tile * TILE, TILE)], act_hbm.at[pl.ds(tile * TILE, TILE)])
+
+    for half in range(2):
+        dense(2 * rep + half)
+        for m, q in enumerate(behind):
+            own, theirs = agg.at[2 * rep + half], agg.at[2 * q + half]
+            remote(own, theirs, s2.at[half, m], r2.at[half, m], (q, blk)).wait_recv()
+            dense(2 * q + half)
 
 
     slab = wsum[pl.ds(pl.multiple_of(rep * 16, 16), 16), :]
@@ -315,7 +316,9 @@
         tile = 2 * (zt * 4 + x * 2 + c)
         return sums[plan[3, tile]], sums[plan[3, tile + 1]]
 
-    w2_copies = []
+    def sum_along_z(source, slot, distance):
+        return remote(source, w2.at[slot], w2s.at[slot], w2r.at[slot], at_z(distance))
+
     core_copies = {}
     x_copies = {}
 
@@ -353,50 +356,83 @@
             core_copies[j, h] = start(
                 remote(to_core.at[j, h], from_core.at[j, h], ds.at[j, h], dr.at[j, h], sibling)
             )
-        if j == 0:
+        if j:
+            send_across(j - 1)
+        if j == 1:
             for copy in w1_copies:
                 copy.wait_recv()
             w2own[...] = grads[low] + w1[1] + w1[2] + w1[3]
-            w2_copies = [
-                start(remote(w2own, w2.at[k], w2s.at[k], w2r.at[k], at_z(k))) for k in range(1, NZ)
-            ]
-        if j:
-            send_across(j - 1)
+            for slot, distance in ((2, 2), (6, -2), (1, 1), (7, -1)):
+                start(sum_along_z(w2own, slot, distance))
     send_across(3)
-
+    sum_along_z(w2own, 2, 1).wait_recv()
+    start(sum_along_z(w2.at[2], 3, 1))
+    sum_along_z(w2own, 6, 1).wait_recv()
+    start(sum_along_z(w2.at[6], 5, -1))
+    start(sum_along_z(w2.at[2 + 4 * core], 4, 2 - 4 * core))
+
+
+    odd = flip == 1
+    where_is = {4: (0, 1), 2: (1, 1), -2: (2, 1), 0: (3, 1)}
+    where_is[3] = jnp.where(odd, 0, 1), 0
+    where_is[-3] = jnp.where(odd, 2, 0), 0
+    where_is[1] = jnp.where(odd, 1, 3), 0
+    where_is[-1] = jnp.where(odd, 3, 2), 0
+
+    def summed_for(k):
+        j, h = where_is[k]
+        remote(to_x.at[j, h], from_x.at[j, h], xs.at[j, h], xr.at[j, h], across).wait_recv()
+        a, b = sum_of(wrap(z + k, NZ), xl, core)
+        a = a + from_core[j, h, xl, 0].astype(F32) + from_x[j, h, 0].astype(F32)
+        b = b + from_core[j, h, xl, 1].astype(F32) + from_x[j, h, 1].astype(F32)
+        return a, b
+
+    Z_SLOT = {4: 0, 3: 1, -3: 2, 2: 3, -2: 4, 1: 5, -1: 6}
+
+    def hop(k, distance):
+        n = Z_SLOT[k]
+        return remote(to_z.at[n], from_z.at[n], es.at[n], er.at[n], at_z(distance))
+
+    def send_along(k, parts, distance):
+        n = Z_SLOT[k]
+        to_z[n, 0] = parts[0].astype(BF16)
+        to_z[n, 1] = parts[1].astype(BF16)
+        start(hop(k, distance))
+
+    def passed_on(k):
+        hop(k, 1).wait_recv()
+        return from_z[Z_SLOT[k], 0].astype(F32), from_z[Z_SLOT[k], 1].astype(F32)
+
+    send_along(4, summed_for(4), 2 - 4 * core)
+    send_along(3, summed_for(3), 2)
+    send_along(-3, summed_for(-3), -2)
+
+    for slot in (1, 7, 3, 5, 4):
+        sum_along_z(w2own, slot, 1).wait_recv()
     summed = w2own[...]
-    for i, copy in enumerate(w2_copies):
-        copy.wait_recv()
-        summed += w2[i + 1]
+    for slot in range(1, NZ):
+        summed += w2[slot]
     w3[rep] = summed[0:8]
     bgrad_ref[:, 0:128] = jnp.sum(summed[8:16], axis=0, keepdims=True)
     bgrad_ref[:, 128:256] = jnp.sum(summed[16:24], axis=0, keepdims=True)
     for m, q in enumerate(ahead):
         start(remote(w3.at[rep], w3.at[rep], w3s.at[m], w3r.at[m], (q, blk)))
 
-    z_copies = {}
-    kept = None
-    for j in range(4):
-        for h in range(2):
-            zt = halves[j][h]
-            x_copies[j, h].wait_recv()
-            a, b = sum_of(zt, xl, core)
-            a = a + from_core[j, h, xl, 0].astype(F32) + from_x[j, h, 0].astype(F32)
-            b = b + from_core[j, h, xl, 1].astype(F32) + from_x[j, h, 1].astype(F32)
-            if (j, h) == (3, 1):
-                kept = (a, b)
-            else:
-                k = wrap(zt - z, NZ)
-                to_z[j, h, 0] = a.astype(BF16)
-                to_z[j, h, 1] = b.astype(BF16)
-                z_copies[j, h] = start(
-                    remote(to_z.at[j, h], from_z.at[k], es.at[k], er.at[k], (rep, zt * 4 + low))
-                )
-        if j == 1:
-            for m, q in enumerate(behind):
-                remote(w3.at[rep], w3.at[q], w3s.at[m], w3r.at[m], (q, blk)).wait_recv()
-            for i in range(1, 4):
-                start(remote(w3, w4.at[i], w4s.at[i], w4r.at[i], lows[i - 1]))
+    far = passed_on(4)
+    for k, holder in ((2, 0), (-2, 1)):
+        a, b = summed_for(k)
+        mine = core == holder
+        send_along(k, (a + jnp.where(mine, far[0], 0.0), b + jnp.where(mine, far[1], 0.0)), k)
+    for k in (1, -1):
+        a, b = summed_for(k)
+        c, d = passed_on(3 * k)
+        send_along(k, (a + c, b + d), k)
+    kept = summed_for(0)
+
+    for m, q in enumerate(behind):
+        remote(w3.at[rep], w3.at[q], w3s.at[m], w3r.at[m], (q, blk)).wait_recv()
+    for i in range(1, 4):
+        start(remote(w3, w4.at[i], w4s.at[i], w4r.at[i], lows[i - 1]))
 
     def put(which, source):
         up, side = which // 2, lax.rem(which, 2)
@@ -408,20 +444,19 @@
                     wgrad_ref[pl.ds(pl.multiple_of(q * 16 + up * 8, 8), 8), s * 128 : (s + 1) * 128] = source[q]
 
     put(low, w3)
+    a, b = kept
+    for k in (2, -2, 1, -1):
+        c, d = passed_on(k)
+        a += c
+        b += d
+    feature_ref[0:TILE, :] = a.T
+    feature_ref[TILE : 2 * TILE, :] = b.T
+    store_part(18, feature_ref, feature_hbm)
     for i in range(1, 4):
         remote(w3, w4.at[i], w4s.at[i], w4r.at[i], lows[i - 1]).wait_recv()
         put(wrap(low - i, 4), w4.at[i])
-    store_part(8, wgrad_ref, wgrad_hbm)
-    store_part(9, bgrad_ref, bgrad_hbm)
-
-    a, b = kept
-    for k in (4, 3, 5, 2, 6, 1, 7):
-        remote(to_z.at[0, 0], from_z.at[k], es.at[k], er.at[k], at_z(k)).wait_recv()
-        a += from_z[k, 0].astype(F32)
-        b += from_z[k, 1].astype(F32)
-    feature_ref[0:TILE, :] = a.T
-    feature_ref[TILE : 2 * TILE, :] = b.T
-    store_part(10, feature_ref, feature_hbm)
+    store_part(16, wgrad_ref, wgrad_hbm)
+    store_part(17, bgrad_ref, bgrad_hbm)
     for copy in started:
         copy.wait_send()
     for piece, slot, group in pieces:
@@ -465,8 +500,8 @@
             pltpu.VMEM((SLOTS + 1, TILE, F), F32),
             pltpu.VMEM((8, 128), jnp.int32),
             pltpu.SMEM((8, 128), jnp.int32),
-            pltpu.VMEM((REP - 1,) + tiles, BF16),
-            pltpu.VMEM((REP - 1,) + tiles, BF16),
+            pltpu.VMEM((2, REP - 1, TILE, F), BF16),
+            pltpu.VMEM((2, REP - 1, TILE, F), BF16),
             pltpu.VMEM((PER_SIDE, TILE, F), BF16),
             pltpu.VMEM((PER_SIDE, F, TILE), BF16),
             pltpu.VMEM((F, H), F32),
@@ -476,7 +511,7 @@
             pltpu.VMEM((4, 2, 2) + tiles, BF16),
             pltpu.VMEM((4, 2) + tiles, BF16),
             pltpu.VMEM((4, 2) + tiles, BF16),
-            pltpu.VMEM((4, 2) + tiles, BF16),
+            pltpu.VMEM((NZ,) + tiles, BF16),
             pltpu.VMEM((NZ,) + tiles, BF16),
             pltpu.VMEM((4, 24, 128), F32),
             pltpu.VMEM((24, 128), F32),
@@ -484,17 +519,17 @@
             pltpu.VMEM((REP, 8, 128), F32),
             pltpu.VMEM((4, REP, 8, 128), F32),
             DMA((9,)),
-            DMA((11,)),
+            DMA((19,)),
             DMA((NZ,)),
             DMA((NZ,)),
             DMA((16,)),
             DMA((16,)),
             DMA((16,)),
             DMA((16,)),
-            DMA((REP - 1,)),
-            DMA((REP - 1,)),
-            DMA((REP - 1,)),
-            DMA((REP - 1,)),
+            DMA((2, REP - 1)),
+            DMA((2, REP - 1)),
+            DMA((2, REP - 1)),
+            DMA((2, REP - 1)),
             DMA((4, 2)),
             DMA((4, 2)),
             DMA((4, 2)),

time: 85.7 us -> 79.1 us (0.923)
  the two profiles are of different devices: /device:TPU:32 before, /device:TPU:1 now
where the time goes in v3:
time: 79.1 us; the launch traced here: 79 us
  Pallas kernels  78.4 us (99%)
    pallas_call x1, Pallas kernels, layer(): pl.pallas_call(layer_kernel, out_shape=(jax.ShapeDtypeStruct((SLAB, H), B...  76.2 us
    pallas_call x1, Pallas kernels, store(): pl.pallas_call(store_kernel, out_shape=tuple((jax.ShapeDtypeStruct(a.shap...  2.12 us

profile of v3, /device:TPU:1, one launch (start us, length us, event | category | flops | bytes accessed | tf_op | source)
XLA Modules:
  0.0 79.0 jit_solution(2300937188316515858)
XLA Ops:
  0.6 76.2 %layer.1 = (bf16[2048,256]{1,0:T(8,128)(2,1)}, f32[256,128]{1,0:T(8,128)}, f32[128,256]{1,0:T(8,128)}, f32[1,256]{1,0:T(1,128)}) custom-call(bf16[2,128,128]{2,1,0:T(8,128)(2,1)} %bitcast.5, bf16[128,256]{1,0:T(8,128)(2,1)} %weight_hbm.1, f32[1,256]{1,0:T(1,128)} %bitcast.6, s32[1,4,16]{2,1,0:T(4,128)} %rows_hbm.1, s32[1,4,16]{2,1,0:T(4,128)} %cols_hbm.1, ...), custom_call_target="tpu_custom_call" | custom-call | tf_op jit(solution)/shard_map/layer/pallas_call | solution.py:475
  76.9 2.1 %store.1 = (bf16[2048,256]{1,0:T(8,128)(2,1)}, f32[256,128]{1,0:T(8,128)}, f32[128,256]{1,0:T(8,128)}, f32[1,256]{1,0:T(1,128)}) custom-call(bf16[2048,256]{1,0:T(8,128)(2,1)} %get-tuple-element.12.act_in, f32[256,128]{1,0:T(8,128)} %get-tuple-element.13.feature_in, f32[128,256]{1,0:T(8,128)} %get-tuple-element.14.wgrad_in, f32[1,256]{1,0:T(1,128)} %get-tuple-element.15.bgrad_in), custom_call_target="tpu_custom_call" | custom-call | tf_op jit(solution)/shard_map/store/pallas_call | solution.py:574

commit v4 on v3

--- a/solution.py
+++ b/solution.py
@@ -93,7 +93,7 @@
     load_adj = load(4, adj_hbm, adj)
     load_dense = [load(5, cot_hbm, cot), load(6, weight_hbm, weight_ref), load(7, bias_hbm, bias_ref)]
 
-    peers = [at_z(k) for k in (2, -2, 1, -1)] + lows
+    peers = [at_z(k) for k in range(1, NZ)] + lows
     peers += [(q, z * 4 + x * 2 + core) for q in ahead for x in range(2)]
     meet(peers)
 
@@ -103,6 +103,25 @@
         copy.start()
         started.append(copy)
         return copy
+
+    def settle_early():
+        settle(rep_sends)
+        for copy in stores:
+            copy.wait()
+        stores.clear()
+
+    def settle(copies):
+        for copy in list(copies):
+            copy.wait_send()
+            started.remove(copy)
+        for piece, slot, group in pieces:
+            for to_xl in range(2):
+
+                @pl.when(jnp.logical_not((group == rep) & (xl == to_xl)))
+                def _():
+                    in_plane(piece, slot, group, to_xl).wait_send()
+
+        pieces.clear()
 
 
     def along_z(source, slot, step):
@@ -243,6 +262,8 @@
     for turn in range(2, 4):
         forward(there, turn)
 
+    gather_sends = list(started)
+    rep_sends = []
     scatter = {}
     for half in range(2):
         for m, q in enumerate(ahead):
@@ -250,6 +271,8 @@
             scatter[half, m] = start(
                 remote(to_rep.at[half, m], inbox.at[half, m], s1.at[half, m], r1.at[half, m], (q, blk))
             )
+            rep_sends.append(scatter[half, m])
+    settle(gather_sends)
     for half in range(2):
         total = sums[plan[1, 2 * rep + half]]
         for m in range(REP - 1):
@@ -258,7 +281,7 @@
         agg[2 * rep + half] = total.astype(BF16)
         for m, q in enumerate(ahead):
             own = agg.at[2 * rep + half]
-            start(remote(own, own, s2.at[half, m], r2.at[half, m], (q, blk)))
+            rep_sends.append(start(remote(own, own, s2.at[half, m], r2.at[half, m], (q, blk))))
 
 
     wsum[...] = jnp.zeros_like(wsum)
@@ -362,15 +385,10 @@
             for copy in w1_copies:
                 copy.wait_recv()
             w2own[...] = grads[low] + w1[1] + w1[2] + w1[3]
-            for slot, distance in ((2, 2), (6, -2), (1, 1), (7, -1)):
-                start(sum_along_z(w2own, slot, distance))
+            for slot in (4, 3, 5, 2, 6, 1, 7):
+                start(sum_along_z(w2own, slot, slot))
     send_across(3)
-    sum_along_z(w2own, 2, 1).wait_recv()
-    start(sum_along_z(w2.at[2], 3, 1))
-    sum_along_z(w2own, 6, 1).wait_recv()
-    start(sum_along_z(w2.at[6], 5, -1))
-    start(sum_along_z(w2.at[2 + 4 * core], 4, 2 - 4 * core))
-
+    settle_early()
 
     odd = flip == 1
     where_is = {4: (0, 1), 2: (1, 1), -2: (2, 1), 0: (3, 1)}
@@ -404,10 +422,7 @@
         return from_z[Z_SLOT[k], 0].astype(F32), from_z[Z_SLOT[k], 1].astype(F32)
 
     send_along(4, summed_for(4), 2 - 4 * core)
-    send_along(3, summed_for(3), 2)
-    send_along(-3, summed_for(-3), -2)
-
-    for slot in (1, 7, 3, 5, 4):
+    for slot in range(1, NZ):
         sum_along_z(w2own, slot, 1).wait_recv()
     summed = w2own[...]
     for slot in range(1, NZ):
@@ -418,21 +433,23 @@
     for m, q in enumerate(ahead):
         start(remote(w3.at[rep], w3.at[rep], w3s.at[m], w3r.at[m], (q, blk)))
 
+    send_along(3, summed_for(3), 2)
+    send_along(-3, summed_for(-3), -2)
+
     far = passed_on(4)
     for k, holder in ((2, 0), (-2, 1)):
         a, b = summed_for(k)
         mine = core == holder
         send_along(k, (a + jnp.where(mine, far[0], 0.0), b + jnp.where(mine, far[1], 0.0)), k)
+    for m, q in enumerate(behind):
+        remote(w3.at[rep], w3.at[q], w3s.at[m], w3r.at[m], (q, blk)).wait_recv()
+    for i in range(1, 4):
+        start(remote(w3, w4.at[i], w4s.at[i], w4r.at[i], lows[i - 1]))
     for k in (1, -1):
         a, b = summed_for(k)
         c, d = passed_on(3 * k)
         send_along(k, (a + c, b + d), k)
     kept = summed_for(0)
-
-    for m, q in enumerate(behind):
-        remote(w3.at[rep], w3.at[q], w3s.at[m], w3r.at[m], (q, blk)).wait_recv()
-    for i in range(1, 4):
-        start(remote(w3, w4.at[i], w4s.at[i], w4r.at[i], lows[i - 1]))
 
     def put(which, source):
         up, side = which // 2, lax.rem(which, 2)
@@ -457,15 +474,7 @@
         put(wrap(low - i, 4), w4.at[i])
     store_part(16, wgrad_ref, wgrad_hbm)
     store_part(17, bgrad_ref, bgrad_hbm)
-    for copy in started:
-        copy.wait_send()
-    for piece, slot, group in pieces:
-        for to_xl in range(2):
-
-            @pl.when(jnp.logical_not((group == rep) & (xl == to_xl)))
-            def _():
-                in_plane(piece, slot, group, to_xl).wait_send()
-
+    settle(started)
     for copy in stores:
         copy.wait()
 

time: 79.1 us -> 79.2 us (level)
  no operation moved by 1% of the time
where the time goes in v4:
time: 79.2 us; the launch traced here: 79.1 us
  Pallas kernels  78.5 us (99%)
    pallas_call x1, Pallas kernels, layer(): pl.pallas_call(layer_kernel, out_shape=(jax.ShapeDtypeStruct((SLAB, H), B...  76.4 us
    pallas_call x1, Pallas kernels, store(): pl.pallas_call(store_kernel, out_shape=tuple((jax.ShapeDtypeStruct(a.shap...  2.12 us

profile of v4, /device:TPU:1, one launch (start us, length us, event | category | flops | bytes accessed | tf_op | source)
XLA Modules:
  0.0 79.1 jit_solution(16331799484268314617)
XLA Ops:
  0.6 76.4 %layer.1 = (bf16[2048,256]{1,0:T(8,128)(2,1)}, f32[256,128]{1,0:T(8,128)}, f32[128,256]{1,0:T(8,128)}, f32[1,256]{1,0:T(1,128)}) custom-call(bf16[2,128,128]{2,1,0:T(8,128)(2,1)} %bitcast.5, bf16[128,256]{1,0:T(8,128)(2,1)} %weight_hbm.1, f32[1,256]{1,0:T(1,128)} %bitcast.6, s32[1,4,16]{2,1,0:T(4,128)} %rows_hbm.1, s32[1,4,16]{2,1,0:T(4,128)} %cols_hbm.1, ...), custom_call_target="tpu_custom_call" | custom-call | tf_op jit(solution)/shard_map/layer/pallas_call | solution.py:484
  77.0 2.1 %store.1 = (bf16[2048,256]{1,0:T(8,128)(2,1)}, f32[256,128]{1,0:T(8,128)}, f32[128,256]{1,0:T(8,128)}, f32[1,256]{1,0:T(1,128)}) custom-call(bf16[2048,256]{1,0:T(8,128)(2,1)} %get-tuple-element.12.act_in, f32[256,128]{1,0:T(8,128)} %get-tuple-element.13.feature_in, f32[128,256]{1,0:T(8,128)} %get-tuple-element.14.wgrad_in, f32[1,256]{1,0:T(1,128)} %get-tuple-element.15.bgrad_in), custom_call_target="tpu_custom_call" | custom-call | tf_op jit(solution)/shard_map/store/pallas_call | solution.py:583
